TPU v7x, 256 devices: a whole 4x4x8 slice. The times are simulated.
256 devices in a mesh: gz: 64 (over x, z, core), gy: 4 (over y).
Axes of the slice: x: 4, y: 4, z: 8, core: 2. Of those that a mesh axis runs over, the one named last changes fastest.
Arguments:
- velocity: float32 [3, 128, 8, 128], P(None, 'gz', 'gy'), may hold values from -6 to 6
- slip: float32 [3, 131072], P(None, ('gz', 'gy')), may hold values from -6 to 6
- rate: float32 [131072], P(('gz', 'gy')), may hold values from 0.5 to 4
- owner: int32 [131072, 1], P(('gz', 'gy')), may hold values from 0 to 63; in each aligned block of 512 rows (0 to 511, 512 to 1023, ...) at most 16 rows name the same one
- cell: int32 [131072], P(('gz', 'gy')), may hold values from 0 to 511
- count: int32 [256], P(('gz', 'gy')), may hold values from 256 to 512
- w_in: bfloat16 [12, 1024], replicated, may hold values from -1.75 to 1.75
- b_in: float32 [1024], replicated, may hold values from -3 to 3
- w_mid: bfloat16 [1024, 1024], replicated, may hold values from -0.1875 to 0.1875
- b_mid: float32 [1024], replicated, may hold values from -3 to 3
- w_out: bfloat16 [1024, 6], replicated, may hold values from -0.1875 to 0.1875
- tau_bar: bfloat16 [6, 128, 8, 128], P(None, 'gz', 'gy'), may hold values from -1.5 to 1.5
Outputs:
- stress: float32 [6, 128, 8, 128], P(None, 'gz', 'gy')
- velocity_bar: float32 [3, 128, 8, 128], P(None, 'gz', 'gy')
- slip_bar: float32 [3, 131072], P(None, ('gz', 'gy'))
- rate_bar: float32 [131072], P(('gz', 'gy'))
- grad_w_in: float32 [12, 1024], replicated
- grad_b_in: float32 [1024], replicated
- grad_w_mid: float32 [1024, 1024], replicated
- grad_b_mid: float32 [1024], replicated
- grad_w_out: float32 [1024, 6], replicated
Inputs may be any that keep to these rules, and one draw needn't show every extreme that they name: Each particle's cell lies in the slab owner names, in the y-range of the particle's own device index along gy. Among the 512 slots of one device, at most 16 name the same slab, and that many do for some slab. The cell is flattened in the order z, y, x of the owner's block. The first count slots of a device are live, the others empty.
All inputs are finite; a program needn't handle non-finite values.
Results may differ from a plain program's by a relative error of at most 0.007.
Values sent between devices are 32-bit elements; how exact they have to be, the bound alone decides.
A program may use at most 64 MiB of HBM per device.

v0:
```python
import jax
import jax.numpy as jnp
from jax import lax
from jax.sharding import PartitionSpec as P


def with_halo(cells, sides, width):
    for axis, dim in sides:
        count = lax.axis_size(axis)
        head = lax.slice_in_dim(cells, 0, width, axis=dim)
        tail = lax.slice_in_dim(cells, cells.shape[dim] - width, cells.shape[dim], axis=dim)
        cells = jnp.concatenate(
            [
                lax.ppermute(tail, axis, [(i, (i + 1) % count) for i in range(count)]),
                cells,
                lax.ppermute(head, axis, [((i + 1) % count, i) for i in range(count)]),
            ],
            axis=dim,
        )
    return cells


def dsilu(value):
    sig = jax.nn.sigmoid(value)
    return sig * (1.0 + value * (1.0 - sig))


def deposit(forces, cell_row, ncells):
    block = min(512, ncells)
    count_blocks = ncells // block

    def deposit_one_block(index):
        start = index * block
        onehot = (
            cell_row[0][:, None] == start + jnp.arange(block, dtype=jnp.int32)[None, :]
        ).astype(jnp.float32)
        return jnp.dot(
            forces, onehot, precision=lax.Precision.HIGHEST, preferred_element_type=jnp.float32
        )

    pieces = lax.map(deposit_one_block, jnp.arange(count_blocks, dtype=jnp.int32))
    return pieces.transpose(1, 0, 2).reshape(forces.shape[0], ncells)


def collect(values, cell_row, ncells):
    block = min(512, ncells)
    count_blocks = ncells // block

    def collect_one_block(index, total):
        start = index * block
        onehot = (
            start + jnp.arange(block, dtype=jnp.int32)[:, None] == cell_row[0][None, :]
        ).astype(jnp.float32)
        return total + jnp.dot(
            values, onehot, precision=lax.Precision.HIGHEST, preferred_element_type=jnp.float32
        )

    init = jnp.zeros((values.shape[0], cell_row.shape[1]), jnp.float32)
    return lax.fori_loop(0, count_blocks, collect_one_block, init)


def roll_diff(field):
    return (jnp.roll(field, -1, 3) - jnp.roll(field, 1, 3)) * 0.5


def shards(velocity, slip, rate, owner, cell, count, w_in, b_in, w_mid, b_mid, w_out, tau_bar):
    nparts = slip.shape[1]
    slabs = lax.axis_size("gz")
    capacity = 2 * nparts // slabs
    width_all = slabs * capacity
    ncz, ncy, ncx = (velocity.shape[1], velocity.shape[2], velocity.shape[3])
    ncells = ncz * ncy * ncx
    padded = with_halo(velocity, (("gz", 1), ("gy", 2)), 1)
    core = padded[:, 1:-1, 1:-1]
    along_z = (padded[:, 2:, 1:-1] - padded[:, :-2, 1:-1]) * 0.5
    along_y = (padded[:, 1:-1, 2:] - padded[:, 1:-1, :-2]) * 0.5
    grads = jnp.stack([along_z, along_y, roll_diff(core)], 1).reshape(9, ncells)
    live = jnp.arange(nparts, dtype=jnp.int32) < count[0]
    force = jnp.where(live[None, :], rate[None, :] * slip, 0.0)
    owners = owner[:, 0]
    member = (owners[:, None] == jnp.arange(slabs, dtype=jnp.int32)[None, :]).astype(jnp.int32)
    before = jnp.cumsum(member, 0) - member
    position = jnp.sum(before * member, 1)
    slot = owners * capacity + position
    send_force = jnp.zeros((3, width_all), jnp.float32).at[:, slot].set(force)
    send_cell = jnp.full((1, width_all), -1, jnp.int32).at[0, slot].set(jnp.where(live, cell, -1))
    recv_force, recv_cell = (
        lax.all_to_all(send_force, "gz", split_axis=1, concat_axis=1, tiled=True),
        lax.all_to_all(send_cell, "gz", split_axis=1, concat_axis=1, tiled=True),
    )
    source = deposit(recv_force, recv_cell, ncells)
    feats = jnp.concatenate([grads, source], 0).astype(jnp.bfloat16)
    tbar = tau_bar.reshape(tau_bar.shape[0], ncells)
    pre1 = jnp.einsum("fh,fc->hc", w_in, feats, preferred_element_type=jnp.float32) + b_in[:, None]
    hidden_one = jax.nn.silu(pre1).astype(jnp.bfloat16)
    pre2 = (
        jnp.einsum("gh,gc->hc", w_mid, hidden_one, preferred_element_type=jnp.float32)
        + b_mid[:, None]
    )
    hidden_two = jax.nn.silu(pre2).astype(jnp.bfloat16)
    stress = jnp.einsum("ho,hc->oc", w_out, hidden_two, preferred_element_type=jnp.float32)
    grad_w_out = jnp.einsum("hc,oc->ho", hidden_two, tbar, preferred_element_type=jnp.float32)
    back_two = jnp.einsum("ho,oc->hc", w_out, tbar, preferred_element_type=jnp.float32)
    delta_two = (back_two * dsilu(pre2)).astype(jnp.bfloat16)
    grad_w_mid = jnp.einsum("gc,hc->gh", hidden_one, delta_two, preferred_element_type=jnp.float32)
    grad_b_mid = jnp.sum(delta_two.astype(jnp.float32), 1)
    back_one = jnp.einsum("gh,hc->gc", w_mid, delta_two, preferred_element_type=jnp.float32)
    delta_one = (back_one * dsilu(pre1)).astype(jnp.bfloat16)
    grad_w_in = jnp.einsum("fc,hc->fh", feats, delta_one, preferred_element_type=jnp.float32)
    grad_b_in = jnp.sum(delta_one.astype(jnp.float32), 1)
    grad_w_in, grad_b_in, grad_w_mid, grad_b_mid, grad_w_out = lax.psum(
        (grad_w_in, grad_b_in, grad_w_mid, grad_b_mid, grad_w_out), ("gz", "gy")
    )
    feats_bar = jnp.einsum("fh,hc->fc", w_in, delta_one, preferred_element_type=jnp.float32)
    grads_bar = feats_bar[:9].reshape(3, 3, ncz, ncy, ncx)
    joint = with_halo(grads_bar.reshape(9, ncz, ncy, ncx), (("gz", 1), ("gy", 2)), 1)
    joint = joint.reshape(3, 3, ncz + 2, ncy + 2, ncx)
    term_z = (joint[:, 0, 2:, 1:-1] - joint[:, 0, :-2, 1:-1]) * 0.5
    term_y = (joint[:, 1, 1:-1, 2:] - joint[:, 1, 1:-1, :-2]) * 0.5
    term_x = roll_diff(joint[:, 2, 1:-1, 1:-1])
    velocity_bar = -(term_z + term_y + term_x)
    source_bar = feats_bar[9:12]
    per_slot = collect(source_bar, recv_cell, ncells)
    returned = lax.all_to_all(per_slot, "gz", split_axis=1, concat_axis=1, tiled=True)
    at_particle = returned[:, slot]
    slip_bar = jnp.where(live[None, :], rate[None, :] * at_particle, 0.0)
    rate_bar = jnp.where(live, jnp.sum(slip * at_particle, 0), 0.0)
    return (
        stress.reshape(stress.shape[0], ncz, ncy, ncx),
        velocity_bar,
        slip_bar,
        rate_bar,
        grad_w_in,
        grad_b_in,
        grad_w_mid,
        grad_b_mid,
        grad_w_out,
    )


def solution(mesh):
    return jax.shard_map(
        shards,
        mesh=mesh,
        in_specs=(
            P(None, "gz", "gy", None),
            P(None, ("gz", "gy")),
            P(("gz", "gy")),
            P(("gz", "gy"), None),
            P(("gz", "gy")),
            P(("gz", "gy")),
            P(),
            P(),
            P(),
            P(),
            P(),
            P(None, "gz", "gy", None),
        ),
        out_specs=(
            P(None, "gz", "gy", None),
            P(None, "gz", "gy", None),
            P(None, ("gz", "gy")),
            P(("gz", "gy")),
            P(),
            P(),
            P(),
            P(),
            P(),
        ),
        check_vma=False,
    )
```

profile of v0, /device:TPU:2, one launch (start us, length us, event | category | flops | bytes accessed | tf_op | source)
XLA Modules:
  0.0 601.2 jit_solution(1143076900839981350)
XLA Ops:
  7.2 0.9 fusion.62
  8.0 5.3 collective-permute-start
  14.0 0.7 fusion.28
  14.7 1.2 reduce-window.6
  16.2 0.8 fusion.27
  17.0 0.7 compare_select_fusion
  17.7 0.7 broadcast_select_fusion.1
  18.3 2.4 scatter_custom_fusion.1
  20.8 0.7 all_to_all.25
  21.5 9.7 %all-to-all-start.1 = ((s32[1,64,16]{2,0,1:T(1,128)}), s32[1,64,16]{2,0,1:T(1,128)S(1)}, u32[]{:S(2)}, u32[]{:S(2)}) async-start(s32[1,64,16]{2,0,1:T(1,128)} %bitcast.14), calls=%async_computation.1 | async-start | bytes 65536 | tf_op jit(solution)/shard_map/all_to_all | solution.py:89
  31.1 0.8 slice_bitcast_fusion.5
  32.0 0.8 fusion.63
  32.8 0.7 multiply_select_fusion
  34.0 0.8 fusion.47
  34.8 3.1 collective-permute-start.2
  38.0 0.8 copy.88
  38.9 0.7 reshape.131
  39.7 1.9 scatter_custom_fusion
  41.6 1.1 copy.79
  42.7 10.3 %all-to-all-start = ((f32[3,64,16]{2,0,1:T(4,128)}), f32[3,64,16]{2,0,1:T(4,128)S(1)}, u32[]{:S(2)}, u32[]{:S(2)}) async-start(f32[3,64,16]{2,0,1:T(4,128)} %copy.79), calls=%async_computation | async-start | bytes 262144 | tf_op jit(solution)/shard_map/all_to_all | solution.py:88
  53.8 0.7 reduce.5
  54.7 7.7 %all-to-all-done = f32[3,64,16]{2,0,1:T(4,128)S(1)} async-done(((f32[3,64,16]{2,0,1:T(4,128)}), f32[3,64,16]{2,0,1:T(4,128)S(1)}, u32[]{:S(2)}, u32[]{:S(2)}) %all-to-all-start) | async-done | bytes 12320 | tf_op jit(solution)/shard_map/all_to_all | solution.py:88
  62.6 0.8 fusion.17
  63.9 1.6 fusion.4
  65.9 0.9 fusion.64
  66.7 1.6 convert_reduce_fusion
  68.3 2.4 convert_reduce_fusion.1
  71.1 0.9 fusion.29
  72.0 3.3 fusion.53
  76.1 0.8 fusion.16
  76.9 0.6 reshape.130
  77.5 3.3 collective-permute-start.5
  80.9 0.7 copy.86
  81.6 6.7 %all-to-all-start.2 = ((f32[3,64,16]{2,0,1:T(4,128)}), f32[3,64,16]{2,0,1:T(4,128)S(1)}, u32[]{:S(2)}, u32[]{:S(2)}) async-start(f32[3,64,16]{2,0,1:T(4,128)} %copy.86), calls=%async_computation.2 | async-start | bytes 262144 | tf_op jit(solution)/shard_map/all_to_all | solution.py:124
  88.4 0.7 collective-permute-start.6
  89.1 2.7 collective-permute-start.7
  91.8 5.9 all-to-all-done.2
  98.2 1.0 gather_fusion
  99.6 0.6 broadcast_select_fusion
  100.2 0.7 copy.89
  101.1 0.7 fusion.46
  101.8 212.4 %all-reduce.7.cloned.1.call-done = (f32[12,1024]{1,0:T(8,128)}, f32[1024]{0:T(1024)}, f32[1024]{0:T(1024)}, f32[1024,6]{0,1:T(8,128)}) async-done(((f32[12,1024]{1,0:T(8,128)}, f32[1024]{0:T(1024)}, f32[1024]{0:T(1024)}, f32[1024,6]{0,1:T(8,128)}), (f32[12,1024]{1,0:T(8,128)}, f32[1024]{0:T(1024)}, f32[1024]{0:T(1024)}, f32[1024,6]{0,1:T(8,128)})) %all-reduce.7.cloned.1.call-update) | async-done | bytes 81936 | tf_op jit(solution)/shard_map/psum | solution.py:111
  314.1 271.5 %all-reduce.5.cloned.1.call-done = f32[1024,1024]{1,0:T(8,128)} async-done(((f32[1024,1024]{1,0:T(8,128)}), f32[1024,1024]{1,0:T(8,128)}) %all-reduce.5.cloned.1.call-update) | async-done | bytes 4194320 | tf_op jit(solution)/shard_map/psum | solution.py:111
  585.6 1.5 copy.111
  587.1 1.3 copy.112
  588.4 4.8 copy.113
  593.2 0.6 copy.114
  593.8 0.6 copy.115
  (70 shorter events, 5.1 us)
Async XLA Ops:
  7.2 56.7 %copy-start = (bf16[1024,1024]{1,0:T(8,128)(2,1)S(1)}, bf16[1024,1024]{1,0:T(8,128)(2,1)}, u32[]{:S(2)}) copy-start(bf16[1024,1024]{1,0:T(8,128)(2,1)} %param.20) | copy-start | bytes 6291460
  8.0 26.0 %collective-permute-start = (f32[3,1,2,128]{3,2,1,0:T(2,128)S(1)}, f32[3,1,2,128]{3,2,1,0:T(2,128)S(1)}, u32[]{:S(2)}, u32[]{:S(2)}) collective-permute-start(f32[3,1,2,128]{3,2,1,0:T(2,128)S(1)} %get-tuple-element.90), channel_id=1, source_target_pairs={{4,0},{8,4},{12,8},{16,12},{20,16},{24,20},{28,24},{32,28},{36,32}... | collective-permute-start | bytes 9224 | tf_op jit(solution)/shard_map/ppermute | solution.py:16
  13.3 20.7 %collective-permute-start.1 = (f32[3,1,2,128]{3,2,1,0:T(2,128)S(1)}, f32[3,1,2,128]{3,2,1,0:T(2,128)S(1)}, u32[]{:S(2)}, u32[]{:S(2)}) collective-permute-start(f32[3,1,2,128]{3,2,1,0:T(2,128)S(1)} %get-tuple-element.91), channel_id=1, source_target_pairs={{0,4},{4,8},{8,12},{12,16},{16,20},{20,24},{24,28},{28,32},{32,36}... | collective-permute-start | bytes 9224 | tf_op jit(solution)/shard_map/ppermute | solution.py:14
  14.7 48.7 %copy-start.1 = (bf16[12,1024]{1,0:T(8,128)(2,1)S(1)}, bf16[12,1024]{1,0:T(8,128)(2,1)}, u32[]{:S(2)}) copy-start(bf16[12,1024]{1,0:T(8,128)(2,1)} %param.18) | copy-start | bytes 73732
  21.5 21.2 %all-to-all-start.1 = ((s32[1,64,16]{2,0,1:T(1,128)}), s32[1,64,16]{2,0,1:T(1,128)S(1)}, u32[]{:S(2)}, u32[]{:S(2)}) async-start(s32[1,64,16]{2,0,1:T(1,128)} %bitcast.14), calls=%async_computation.1 | async-start | bytes 65536 | tf_op jit(solution)/shard_map/all_to_all | solution.py:89
  34.8 19.8 %collective-permute-start.2 = (f32[3,4,1,128]{3,2,1,0:T(1,128)S(1)}, f32[3,4,1,128]{3,2,1,0:T(1,128)S(1)}, u32[]{:S(2)}, u32[]{:S(2)}) collective-permute-start(f32[3,4,1,128]{3,2,1,0:T(1,128)S(1)} %get-tuple-element.82), channel_id=1, source_target_pairs={{1,0},{2,1},{3,2},{0,3},{5,4},{6,5},{7,6},{4,7},{9,8},{10,9},{11,1... | collective-permute-start | bytes 18440 | tf_op jit(solution)/shard_map/ppermute | solution.py:16
  37.9 16.7 %collective-permute-start.3 = (f32[3,4,1,128]{3,2,1,0:T(1,128)S(1)}, f32[3,4,1,128]{3,2,1,0:T(1,128)S(1)}, u32[]{:S(2)}, u32[]{:S(2)}) collective-permute-start(f32[3,4,1,128]{3,2,1,0:T(1,128)S(1)} %get-tuple-element.83), channel_id=1, source_target_pairs={{0,1},{1,2},{2,3},{3,0},{4,5},{5,6},{6,7},{7,4},{8,9},{9,10},{10,1... | collective-permute-start | bytes 18440 | tf_op jit(solution)/shard_map/ppermute | solution.py:14
  41.6 22.3 %copy-start.6 = (f32[1024]{0:T(1024)S(1)}, f32[1024]{0:T(1024)}, u32[]{:S(2)}) copy-start(f32[1024]{0:T(1024)} %param.21) | copy-start | bytes 12292
  41.6 22.3 %copy-start.7 = (f32[1024]{0:T(1024)S(1)}, f32[1024]{0:T(1024)}, u32[]{:S(2)}) copy-start(f32[1024]{0:T(1024)} %param.19) | copy-start | bytes 12292
  42.7 19.7 %all-to-all-start = ((f32[3,64,16]{2,0,1:T(4,128)}), f32[3,64,16]{2,0,1:T(4,128)S(1)}, u32[]{:S(2)}, u32[]{:S(2)}) async-start(f32[3,64,16]{2,0,1:T(4,128)} %copy.79), calls=%async_computation | async-start | bytes 262144 | tf_op jit(solution)/shard_map/all_to_all | solution.py:88
  53.0 261.1 %all-reduce.7.cloned.1.call-start = ((), (), s32[]{:S(2)}) async-start(), calls=%async_computation.4 | async-start | bytes 212992 | tf_op jit(solution)/shard_map/psum | solution.py:111
  63.9 1.6 copy-start.3
  75.4 510.2 %all-reduce.5.cloned.1.call-start = ((), (), s32[]{:S(2)}) async-start(), calls=%async_computation.3 | async-start | bytes 8388608 | tf_op jit(solution)/shard_map/psum | solution.py:111
  75.5 23.8 %copy-start.4 = (f32[512]{0:T(512)S(1)}, f32[512]{0:T(512)}, u32[]{:S(2)}) copy-start(f32[512]{0:T(512)} %param.14) | copy-start | bytes 6148
  75.5 12.9 %collective-permute-start.4 = (f32[9,1,2,128]{3,2,1,0:T(2,128)S(1)}, f32[9,1,2,128]{3,2,1,0:T(2,128)S(1)}, u32[]{:S(2)}, u32[]{:S(2)}) collective-permute-start(f32[9,1,2,128]{3,2,1,0:T(2,128)S(1)} %get-tuple-element.81), channel_id=1, source_target_pairs={{0,4},{4,8},{8,12},{12,16},{16,20},{20,24},{24,28},{28,32},{32,36}... | collective-permute-start | bytes 27656 | tf_op jit(solution)/shard_map/ppermute | solution.py:14
  77.5 10.9 %collective-permute-start.5 = (f32[9,1,2,128]{3,2,1,0:T(2,128)S(1)}, f32[9,1,2,128]{3,2,1,0:T(2,128)S(1)}, u32[]{:S(2)}, u32[]{:S(2)}) collective-permute-start(f32[9,1,2,128]{3,2,1,0:T(2,128)S(1)} %get-tuple-element.80), channel_id=1, source_target_pairs={{4,0},{8,4},{12,8},{16,12},{20,16},{24,20},{28,24},{32,28},{36,32}... | collective-permute-start | bytes 27656 | tf_op jit(solution)/shard_map/ppermute | solution.py:16
  81.6 16.2 %all-to-all-start.2 = ((f32[3,64,16]{2,0,1:T(4,128)}), f32[3,64,16]{2,0,1:T(4,128)S(1)}, u32[]{:S(2)}, u32[]{:S(2)}) async-start(f32[3,64,16]{2,0,1:T(4,128)} %copy.86), calls=%async_computation.2 | async-start | bytes 262144 | tf_op jit(solution)/shard_map/all_to_all | solution.py:124
  88.4 12.4 %collective-permute-start.6 = (f32[9,4,1,128]{3,2,1,0:T(1,128)S(1)}, f32[9,4,1,128]{3,2,1,0:T(1,128)S(1)}, u32[]{:S(2)}, u32[]{:S(2)}) collective-permute-start(f32[9,4,1,128]{3,2,1,0:T(1,128)S(1)} %get-tuple-element.78), channel_id=1, source_target_pairs={{0,1},{1,2},{2,3},{3,0},{4,5},{5,6},{6,7},{7,4},{8,9},{9,10},{10,1... | collective-permute-start | bytes 55304 | tf_op jit(solution)/shard_map/ppermute | solution.py:14
  89.1 11.8 %collective-permute-start.7 = (f32[9,4,1,128]{3,2,1,0:T(1,128)S(1)}, f32[9,4,1,128]{3,2,1,0:T(1,128)S(1)}, u32[]{:S(2)}, u32[]{:S(2)}) collective-permute-start(f32[9,4,1,128]{3,2,1,0:T(1,128)S(1)} %get-tuple-element.79), channel_id=1, source_target_pairs={{1,0},{2,1},{3,2},{0,3},{5,4},{6,5},{7,6},{4,7},{9,8},{10,9},{11,1... | collective-permute-start | bytes 55304 | tf_op jit(solution)/shard_map/ppermute | solution.py:16
  588.4 4.8 copy-start.5
  588.4 5.4 copy-start.2
Sparse Core Ops, SparseCore 0:
  75.5 238.5 all-reduce.6
  320.2 265.3 all-reduce.4
where the time goes:
time: 602 us; the launch traced here: 601 us
  waiting for transfers between devices  498 us (83%)
  starting transfers between devices  42.2 us (7%)
  local copies, waits for them, and re-layouts  24.4 us (4%)
  between operations  15 us (2%)
  matrix products  13.5 us (2%)
  other arithmetic  8.1 us (1%)
    psum x2, waiting for transfers between devices, shards(): lax.psum((grad_w_in, grad_b_in, grad_w_mid, grad_b_mid, grad_w_out), ('gz...  484 us
    ppermute x4, starting transfers between devices, with_halo(): lax.ppermute(head, axis, [((i + 1) % count, i) for i in range(count)])  14.4 us
  transfers between devices with their start and end apart: 13, of which 4 were waited for; matrix products, arithmetic and copies ran while one was open for 4% of the time, Pallas kernels for 0%

commit v1 on v0

--- a/solution.py
+++ b/solution.py
@@ -109,7 +109,7 @@
     grad_w_in = jnp.einsum("fc,hc->fh", feats, delta_one, preferred_element_type=jnp.float32)
     grad_b_in = jnp.sum(delta_one.astype(jnp.float32), 1)
     grad_w_in, grad_b_in, grad_w_mid, grad_b_mid, grad_w_out = lax.psum(
-        (grad_w_in, grad_b_in, grad_w_mid, grad_b_mid, grad_w_out), ("gz", "gy")
+        lax.psum((grad_w_in, grad_b_in, grad_w_mid, grad_b_mid, grad_w_out), "gz"), "gy"
     )
     feats_bar = jnp.einsum("fh,hc->fc", w_in, delta_one, preferred_element_type=jnp.float32)
     grads_bar = feats_bar[:9].reshape(3, 3, ncz, ncy, ncx)

time: 602 us -> 603 us (level)
    psum x2 -> x4, waiting for transfers between devices: 484 us -> 479 us  [the longest x2 361 us: shards(): lax.psum((grad_w_in, grad_b_in, grad_w_mid, grad_b_mid, grad_w_out), 'gz')]
  transfers between devices with their start and end apart: 13 -> 15, of which waited for: 4 -> 6; matrix products, arithmetic and copies ran while one was open for 4% -> 5% of each run, Pallas kernels for 0% -> 0%
where the time goes in v1:
time: 603 us; the launch traced here: 601 us
  waiting for transfers between devices  493 us (82%)
  starting transfers between devices  43.3 us (7%)
  local copies, waits for them, and re-layouts  25.5 us (4%)
  matrix products  16.5 us (3%)
  between operations  14.8 us (2%)
  other arithmetic  8.1 us (1%)
    psum x2, waiting for transfers between devices, shards(): lax.psum((grad_w_in, grad_b_in, grad_w_mid, grad_b_mid, grad_w_out), 'gz')  361 us
    psum x2, waiting for transfers between devices, shards(): lax.psum(lax.psum((grad_w_in, grad_b_in, grad_w_mid, grad_b_mid, grad_w_o...  119 us
    ppermute x4, starting transfers between devices, with_halo(): lax.ppermute(head, axis, [((i + 1) % count, i) for i in range(count)])  13.9 us
  transfers between devices with their start and end apart: 15, of which 6 were waited for; matrix products, arithmetic and copies ran while one was open for 5% of the time, Pallas kernels for 0%

profile of v1, /device:TPU:2, one launch (start us, length us, event | category | flops | bytes accessed | tf_op | source)
XLA Modules:
  0.0 601.2 jit_solution(1807877798245109083)
XLA Ops:
  7.2 0.9 fusion.62
  8.1 5.3 collective-permute-start
  14.0 0.7 fusion.28
  14.7 1.2 reduce-window.6
  16.2 0.8 fusion.27
  17.0 0.7 compare_select_fusion
  17.7 0.7 broadcast_select_fusion.1
  18.3 2.4 scatter_custom_fusion.1
  20.8 0.7 all_to_all.25
  21.5 9.7 %all-to-all-start.1 = ((s32[1,64,16]{2,0,1:T(1,128)}), s32[1,64,16]{2,0,1:T(1,128)S(1)}, u32[]{:S(2)}, u32[]{:S(2)}) async-start(s32[1,64,16]{2,0,1:T(1,128)} %bitcast.14), calls=%async_computation.1 | async-start | bytes 65536 | tf_op jit(solution)/shard_map/all_to_all | solution.py:89
  31.1 0.8 slice_bitcast_fusion.5
  32.0 0.7 multiply_select_fusion
  32.7 0.8 fusion.63
  34.0 0.8 fusion.47
  34.8 3.1 collective-permute-start.2
  38.0 0.7 reshape.131
  38.9 1.9 scatter_custom_fusion
  40.8 1.1 copy.79
  41.9 10.3 %all-to-all-start = ((f32[3,64,16]{2,0,1:T(4,128)}), f32[3,64,16]{2,0,1:T(4,128)S(1)}, u32[]{:S(2)}, u32[]{:S(2)}) async-start(f32[3,64,16]{2,0,1:T(4,128)} %copy.79), calls=%async_computation | async-start | bytes 262144 | tf_op jit(solution)/shard_map/all_to_all | solution.py:88
  52.9 0.7 reduce.5
  53.9 7.7 %all-to-all-done = f32[3,64,16]{2,0,1:T(4,128)S(1)} async-done(((f32[3,64,16]{2,0,1:T(4,128)}), f32[3,64,16]{2,0,1:T(4,128)S(1)}, u32[]{:S(2)}, u32[]{:S(2)}) %all-to-all-start) | async-done | bytes 12320 | tf_op jit(solution)/shard_map/all_to_all | solution.py:88
  61.7 0.8 fusion.17
  63.0 1.6 fusion.4
  64.6 0.9 fusion.64
  65.5 1.6 convert_reduce_fusion
  67.1 2.3 convert_reduce_fusion.1
  69.4 1.1 copy-done.1
  70.5 0.9 fusion.29
  71.4 5.2 fusion.53
  76.7 161.9 %all-reduce.12.cloned.1.call-done = (f32[12,1024]{1,0:T(8,128)}, f32[1024]{0:T(1024)}, f32[1024]{0:T(1024)}, f32[1024,6]{0,1:T(8,128)}) async-done(((f32[12,1024]{1,0:T(8,128)}, f32[1024]{0:T(1024)}, f32[1024]{0:T(1024)}, f32[1024,6]{0,1:T(8,128)}), (f32[12,1024]{1,0:T(8,128)}, f32[1024]{0:T(1024)}, f32[1024]{0:T(1024)}, f32[1024,6]{0,1:T(8,128)})) %all-reduce.12.cloned.1.call-update) | async-done | bytes 81936 | tf_op jit(solution)/shard_map/psum | solution.py:112
  238.6 198.9 %all-reduce.8.cloned.1.call-done = f32[1024,1024]{1,0:T(8,128)} async-done(((f32[1024,1024]{1,0:T(8,128)}), f32[1024,1024]{1,0:T(8,128)}) %all-reduce.8.cloned.1.call-update) | async-done | bytes 4194320 | tf_op jit(solution)/shard_map/psum | solution.py:112
  437.5 0.7 copy-done.4
  438.4 1.6 convolution_bitcast_fusion
  440.5 0.8 fusion.16
  441.9 3.8 collective-permute-start.5
  445.8 0.7 copy.86
  446.5 7.4 %all-to-all-start.2 = ((f32[3,64,16]{2,0,1:T(4,128)}), f32[3,64,16]{2,0,1:T(4,128)S(1)}, u32[]{:S(2)}, u32[]{:S(2)}) async-start(f32[3,64,16]{2,0,1:T(4,128)} %copy.86), calls=%async_computation.2 | async-start | bytes 262144 | tf_op jit(solution)/shard_map/all_to_all | solution.py:124
  454.0 1.6 collective-permute-start.6
  455.6 1.8 collective-permute-start.7
  457.4 6.0 all-to-all-done.2
  463.8 1.0 gather_fusion
  465.7 0.7 copy.89
  466.7 0.7 fusion.46
  467.3 17.4 %all-reduce.14.cloned.1.call-done = (f32[12,1024]{1,0:T(8,128)}, f32[1024]{0:T(1024)}, f32[1024]{0:T(1024)}, f32[1024,6]{0,1:T(8,128)}) async-done(((f32[12,1024]{1,0:T(8,128)}, f32[1024]{0:T(1024)}, f32[1024]{0:T(1024)}, f32[1024,6]{0,1:T(8,128)}), (f32[12,1024]{1,0:T(8,128)}, f32[1024]{0:T(1024)}, f32[1024]{0:T(1024)}, f32[1024,6]{0,1:T(8,128)})) %all-reduce.14.cloned.1.call-update) | async-done | bytes 81936 | tf_op jit(solution)/shard_map/psum | solution.py:111
  484.7 101.2 %all-reduce.10.cloned.1.call-done = f32[1024,1024]{1,0:T(8,128)} async-done(((f32[1024,1024]{1,0:T(8,128)}), f32[1024,1024]{1,0:T(8,128)}) %all-reduce.10.cloned.1.call-update) | async-done | bytes 4194320 | tf_op jit(solution)/shard_map/psum | solution.py:111
  585.9 1.5 copy.116
  587.4 1.3 copy.117
  588.7 4.8 copy.118
  (84 shorter events, 6.9 us)
Async XLA Ops:
  7.2 55.8 %copy-start = (bf16[1024,1024]{1,0:T(8,128)(2,1)S(1)}, bf16[1024,1024]{1,0:T(8,128)(2,1)}, u32[]{:S(2)}) copy-start(bf16[1024,1024]{1,0:T(8,128)(2,1)} %param.20) | copy-start | bytes 6291460
  7.2 55.3 %copy-start.3 = (bf16[12,1024]{1,0:T(8,128)(2,1)S(1)}, bf16[12,1024]{1,0:T(8,128)(2,1)}, u32[]{:S(2)}) copy-start(bf16[12,1024]{1,0:T(8,128)(2,1)} %param.18) | copy-start | bytes 73732
  8.1 25.9 %collective-permute-start = (f32[3,1,2,128]{3,2,1,0:T(2,128)S(1)}, f32[3,1,2,128]{3,2,1,0:T(2,128)S(1)}, u32[]{:S(2)}, u32[]{:S(2)}) collective-permute-start(f32[3,1,2,128]{3,2,1,0:T(2,128)S(1)} %get-tuple-element.94), channel_id=1, source_target_pairs={{4,0},{8,4},{12,8},{16,12},{20,16},{24,20},{28,24},{32,28},{36,32}... | collective-permute-start | bytes 9224 | tf_op jit(solution)/shard_map/ppermute | solution.py:16
  13.3 20.7 %collective-permute-start.1 = (f32[3,1,2,128]{3,2,1,0:T(2,128)S(1)}, f32[3,1,2,128]{3,2,1,0:T(2,128)S(1)}, u32[]{:S(2)}, u32[]{:S(2)}) collective-permute-start(f32[3,1,2,128]{3,2,1,0:T(2,128)S(1)} %get-tuple-element.95), channel_id=1, source_target_pairs={{0,4},{4,8},{8,12},{12,16},{16,20},{20,24},{24,28},{28,32},{32,36}... | collective-permute-start | bytes 9224 | tf_op jit(solution)/shard_map/ppermute | solution.py:14
  21.5 20.4 %all-to-all-start.1 = ((s32[1,64,16]{2,0,1:T(1,128)}), s32[1,64,16]{2,0,1:T(1,128)S(1)}, u32[]{:S(2)}, u32[]{:S(2)}) async-start(s32[1,64,16]{2,0,1:T(1,128)} %bitcast.14), calls=%async_computation.1 | async-start | bytes 65536 | tf_op jit(solution)/shard_map/all_to_all | solution.py:89
  34.8 18.9 %collective-permute-start.2 = (f32[3,4,1,128]{3,2,1,0:T(1,128)S(1)}, f32[3,4,1,128]{3,2,1,0:T(1,128)S(1)}, u32[]{:S(2)}, u32[]{:S(2)}) collective-permute-start(f32[3,4,1,128]{3,2,1,0:T(1,128)S(1)} %get-tuple-element.86), channel_id=1, source_target_pairs={{1,0},{2,1},{3,2},{0,3},{5,4},{6,5},{7,6},{4,7},{9,8},{10,9},{11,1... | collective-permute-start | bytes 18440 | tf_op jit(solution)/shard_map/ppermute | solution.py:16
  37.9 15.8 %collective-permute-start.3 = (f32[3,4,1,128]{3,2,1,0:T(1,128)S(1)}, f32[3,4,1,128]{3,2,1,0:T(1,128)S(1)}, u32[]{:S(2)}, u32[]{:S(2)}) collective-permute-start(f32[3,4,1,128]{3,2,1,0:T(1,128)S(1)} %get-tuple-element.87), channel_id=1, source_target_pairs={{0,1},{1,2},{2,3},{3,0},{4,5},{5,6},{6,7},{7,4},{8,9},{9,10},{10,1... | collective-permute-start | bytes 18440 | tf_op jit(solution)/shard_map/ppermute | solution.py:14
  40.7 22.3 %copy-start.9 = (f32[1024]{0:T(1024)S(1)}, f32[1024]{0:T(1024)}, u32[]{:S(2)}) copy-start(f32[1024]{0:T(1024)} %param.21) | copy-start | bytes 12292
  40.7 22.3 %copy-start.10 = (f32[1024]{0:T(1024)S(1)}, f32[1024]{0:T(1024)}, u32[]{:S(2)}) copy-start(f32[1024]{0:T(1024)} %param.19) | copy-start | bytes 12292
  41.9 19.7 %all-to-all-start = ((f32[3,64,16]{2,0,1:T(4,128)}), f32[3,64,16]{2,0,1:T(4,128)S(1)}, u32[]{:S(2)}, u32[]{:S(2)}) async-start(f32[3,64,16]{2,0,1:T(4,128)} %copy.79), calls=%async_computation | async-start | bytes 262144 | tf_op jit(solution)/shard_map/all_to_all | solution.py:88
  52.2 186.4 %all-reduce.12.cloned.1.call-start = ((), (), s32[]{:S(2)}) async-start(), calls=%async_computation.5 | async-start | bytes 212992 | tf_op jit(solution)/shard_map/psum | solution.py:112
  63.0 4.1 copy-start.2
  63.0 2.5 copy-start.6
  67.1 2.3 copy-start.11
  69.4 1.1 copy-start.1
  71.4 366.1 %all-reduce.8.cloned.1.call-start = ((), (), s32[]{:S(2)}) async-start(), calls=%async_computation.3 | async-start | bytes 8388608 | tf_op jit(solution)/shard_map/psum | solution.py:112
  76.7 408.1 %all-reduce.14.cloned.1.call-start = ((), (), s32[]{:S(2)}) async-start(), calls=%async_computation.6 | async-start | bytes 212992 | tf_op jit(solution)/shard_map/psum | solution.py:111
  238.6 347.3 %all-reduce.10.cloned.1.call-start = ((), (), s32[]{:S(2)}) async-start(), calls=%async_computation.4 | async-start | bytes 8388608 | tf_op jit(solution)/shard_map/psum | solution.py:111
  437.5 0.7 copy-start.4
  438.3 26.5 %copy-start.7 = (f32[512]{0:T(512)S(1)}, f32[512]{0:T(512)}, u32[]{:S(2)}) copy-start(f32[512]{0:T(512)} %param.14) | copy-start | bytes 6148
  440.0 13.9 %collective-permute-start.4 = (f32[9,1,2,128]{3,2,1,0:T(2,128)S(1)}, f32[9,1,2,128]{3,2,1,0:T(2,128)S(1)}, u32[]{:S(2)}, u32[]{:S(2)}) collective-permute-start(f32[9,1,2,128]{3,2,1,0:T(2,128)S(1)} %get-tuple-element.85), channel_id=1, source_target_pairs={{0,4},{4,8},{8,12},{12,16},{16,20},{20,24},{24,28},{28,32},{32,36}... | collective-permute-start | bytes 27656 | tf_op jit(solution)/shard_map/ppermute | solution.py:14
  441.9 12.1 %collective-permute-start.5 = (f32[9,1,2,128]{3,2,1,0:T(2,128)S(1)}, f32[9,1,2,128]{3,2,1,0:T(2,128)S(1)}, u32[]{:S(2)}, u32[]{:S(2)}) collective-permute-start(f32[9,1,2,128]{3,2,1,0:T(2,128)S(1)} %get-tuple-element.84), channel_id=1, source_target_pairs={{4,0},{8,4},{12,8},{16,12},{20,16},{24,20},{28,24},{32,28},{36,32}... | collective-permute-start | bytes 27656 | tf_op jit(solution)/shard_map/ppermute | solution.py:16
  446.5 16.8 %all-to-all-start.2 = ((f32[3,64,16]{2,0,1:T(4,128)}), f32[3,64,16]{2,0,1:T(4,128)S(1)}, u32[]{:S(2)}, u32[]{:S(2)}) async-start(f32[3,64,16]{2,0,1:T(4,128)} %copy.86), calls=%async_computation.2 | async-start | bytes 262144 | tf_op jit(solution)/shard_map/all_to_all | solution.py:124
  454.0 12.4 %collective-permute-start.6 = (f32[9,4,1,128]{3,2,1,0:T(1,128)S(1)}, f32[9,4,1,128]{3,2,1,0:T(1,128)S(1)}, u32[]{:S(2)}, u32[]{:S(2)}) collective-permute-start(f32[9,4,1,128]{3,2,1,0:T(1,128)S(1)} %get-tuple-element.82), channel_id=1, source_target_pairs={{0,1},{1,2},{2,3},{3,0},{4,5},{5,6},{6,7},{7,4},{8,9},{9,10},{10,1... | collective-permute-start | bytes 55304 | tf_op jit(solution)/shard_map/ppermute | solution.py:14
  455.6 10.8 %collective-permute-start.7 = (f32[9,4,1,128]{3,2,1,0:T(1,128)S(1)}, f32[9,4,1,128]{3,2,1,0:T(1,128)S(1)}, u32[]{:S(2)}, u32[]{:S(2)}) collective-permute-start(f32[9,4,1,128]{3,2,1,0:T(1,128)S(1)} %get-tuple-element.83), channel_id=1, source_target_pairs={{1,0},{2,1},{3,2},{0,3},{5,4},{6,5},{7,6},{4,7},{9,8},{10,9},{11,1... | collective-permute-start | bytes 55304 | tf_op jit(solution)/shard_map/ppermute | solution.py:16
  588.7 4.8 copy-start.8
  588.7 5.4 copy-start.5
Sparse Core Ops, SparseCore 0:
  71.5 167.0 all-reduce.11
  242.7 194.7 all-reduce.7
  440.2 44.5 all-reduce.13
  486.9 98.9 all-reduce.9
